TPU v7x, 32 devices: a whole 2x2x4 slice. The times are simulated.
32 devices in a mesh: groups: 2 (over y), seq: 4 (over z), dp: 2 (over x), head: 2 (over core).
Axes of the slice: x: 2, y: 2, z: 4, core: 2. Of those that a mesh axis runs over, the one named last changes fastest.
Arguments:
- latents: bfloat16 [4, 8, 512, 1024], P(('groups', 'dp'), None, 'seq', 'head'), parts along dimension 0, may hold values from -6 to 6
- log_decay: bfloat16 [4, 8, 512, 8], P(('groups', 'dp'), None, 'seq', 'head'), parts along dimension 0, may hold values from -1 to 0, as said below
- seg_lengths: int32 [4, 4], P(('groups', 'dp')), parts along dimension 0, may hold values from 1 to 2048, 4096 in all within a row
- qkv_weight: bfloat16 [1024, 3, 1024], P('seq', None, 'head'), may hold values from -0.1875 to 0.1875
- out_weight: bfloat16 [1024, 1024], P('seq', 'head'), may hold values from -0.1875 to 0.1875
- cotangent: bfloat16 [4, 8, 512, 1024], P(('groups', 'dp'), 'seq', None, 'head'), parts along dimension 0, may hold values from -6 to 6
Outputs:
- layer_out: bfloat16 [4, 8, 512, 1024], P(('groups', 'dp'), 'seq', None, 'head'), parts along dimension 0
- output_weight_gradient: float32 [2048, 1024], P(('groups', 'seq'), 'head'), parts along dimension 0
There are 2 independent parts, one for each index of `groups`. A program takes and returns all parts, laid end to end along the dimension named above; an argument that names none is the same for every part. Nothing has to cross between parts.
Inputs may be any that keep to these rules, and one draw needn't show every extreme that they name: `log_decay`: never positive. `seg_lengths`: each row sums to 4096; a segment's state is reset at its first token.
All inputs are finite; a program needn't handle non-finite values.
Results may differ from a plain program's by a relative error of at most 0.0073.
Values may be sent and summed in bfloat16 or wider, within the bound.
A program may use at most 64 MiB of HBM per device.

v0:
```python
from functools import partial
import jax
import jax.numpy as jnp
from jax import lax
from jax.sharding import PartitionSpec as P


def shifted(value, axis, steps):
    count = lax.axis_size(axis)
    initial, last = (max(0, -steps), min(count, count - steps))
    return lax.ppermute(value, axis, [(source, source + steps) for source in range(initial, last)])


def block_step(carry_state, queries, key_rows, values_in, log_rates, segment, previous):
    head_scale = queries.shape[-1] ** (-0.5)
    cumulative = jnp.cumsum(log_rates, axis=-1)
    size_here = log_rates.shape[-1]
    order_idx = jnp.arange(size_here)
    allowed = (order_idx[:, None] >= order_idx[None, :]) & (segment[:, None] == segment[None, :])
    spread = cumulative[:, :, None] - cumulative[:, None, :]
    weight = jnp.where(allowed[None], jnp.exp(jnp.where(allowed[None], spread, 0.0)), 0.0)
    scores = jnp.einsum("htd,hsd->hts", queries, key_rows, preferred_element_type=jnp.float32)
    mixing = (scores * head_scale * weight).astype(jnp.bfloat16)
    inner_sum = jnp.einsum("hts,hsd->htd", mixing, values_in, preferred_element_type=jnp.float32)
    kept_mask = (segment == previous).astype(jnp.float32)
    carried = jnp.einsum(
        "htd,hde->hte", queries.astype(jnp.float32), carry_state, precision=lax.Precision.HIGHEST
    )
    result = (
        inner_sum
        + kept_mask[None, :, None] * jnp.exp(cumulative)[:, :, None] * carried * head_scale
    )
    last_seg = segment[-1]
    tail_decay = (
        jnp.exp(cumulative[:, -1:] - cumulative)
        * (segment == last_seg).astype(jnp.float32)[None, :]
    )
    decayed = (key_rows.astype(jnp.float32) * tail_decay[:, :, None]).astype(jnp.bfloat16)
    fresh = jnp.einsum("hsd,hse->hde", decayed, values_in, preferred_element_type=jnp.float32)
    through = jnp.exp(cumulative[:, -1]) * (last_seg == previous).astype(jnp.float32)
    return (through[:, None, None] * carry_state + fresh, result)


def to_blocks(array, count):
    moved = array.reshape((array.shape[0], count, array.shape[1] // count) + array.shape[2:])
    return jnp.moveaxis(moved, 1, 0)


def local_pass(queries, key_rows, values_in, log_rates, segment, before, block_size):
    heads_here, length, head_dim = queries.shape
    count = length // block_size
    seg_blocks = segment.reshape(count, block_size)
    previous = jnp.concatenate([jnp.reshape(before, (1,)), seg_blocks[:-1, -1]])

    def advance(carry_state, slab_in):
        q_blk, k_blk, v_blk, r_blk, s_blk, p_blk = slab_in
        return block_step(carry_state, q_blk, k_blk, v_blk, r_blk, s_blk, p_blk)

    start_state = jnp.zeros((heads_here, head_dim, head_dim), jnp.float32)
    final_state, block_outs = lax.scan(
        advance,
        start_state,
        (
            to_blocks(queries, count),
            to_blocks(key_rows, count),
            to_blocks(values_in, count),
            to_blocks(log_rates, count),
            seg_blocks,
            previous,
        ),
    )
    outputs = jnp.moveaxis(block_outs, 0, 1).reshape(heads_here, length, head_dim)
    return (outputs, final_state)


def local(latents, log_decay, seg_lengths, qkv_weight, out_weight, cotangent):
    strips, rate_strips = (
        lax.all_to_all(latents, "seq", split_axis=1, concat_axis=2, tiled=True),
        lax.all_to_all(log_decay, "seq", split_axis=1, concat_axis=2, tiled=True),
    )
    features = lax.all_gather(strips, "head", axis=3, tiled=True)
    proj_full, out_full = (
        lax.all_gather(qkv_weight, "seq", axis=0, tiled=True),
        lax.all_gather(out_weight, "seq", axis=0, tiled=True),
    )
    drives_here, rows_here, columns, feature_width = features.shape
    tokens_here = rows_here * columns
    heads_here = rate_strips.shape[3]
    head_dim = proj_full.shape[2] // heads_here
    block_size = min(512, tokens_here)
    split_weight = proj_full.reshape(feature_width, 3, heads_here, head_dim)
    projected = jnp.einsum(
        "bsaf,fchd->cbhsad", features, split_weight, preferred_element_type=jnp.float32
    ).astype(jnp.bfloat16)
    projected = projected.reshape(3, drives_here, heads_here, tokens_here, head_dim)
    log_rates = jnp.transpose(rate_strips.astype(jnp.float32), (0, 3, 1, 2)).reshape(
        drives_here, heads_here, tokens_here
    )
    starts = jnp.cumsum(seg_lengths, axis=1) - seg_lengths
    first_pos = lax.axis_index("seq") * tokens_here
    position = first_pos + jnp.arange(tokens_here, dtype=jnp.int32)
    segment = jnp.sum((starts[:, :, None] <= position[None, None, :]).astype(jnp.int32), axis=1) - 1
    before = jnp.sum((starts <= first_pos - 1).astype(jnp.int32), axis=1) - 1
    run_local = jax.vmap(partial(local_pass, block_size=block_size))
    local_out, own_state = run_local(
        projected[0], projected[1], projected[2], log_rates, segment, before
    )
    running = jnp.cumsum(log_rates, axis=2)
    joined_seg = (segment[:, -1] == before).astype(jnp.float32)
    self_decay = jnp.exp(running[:, :, -1]) * joined_seg[:, None]

    def relay(step_index, incoming):
        return shifted(self_decay[:, :, None, None] * incoming + own_state, "seq", 1)

    prefix = lax.fori_loop(0, lax.axis_size("seq") - 1, relay, jnp.zeros_like(own_state))
    head_scale = head_dim ** (-0.5)
    kept_mask = (segment == before[:, None]).astype(jnp.float32)
    carried = jnp.einsum(
        "bhtd,bhde->bhte", projected[0].astype(jnp.float32), prefix, precision=lax.Precision.HIGHEST
    )
    combined = (
        local_out
        + kept_mask[:, None, :, None] * jnp.exp(running)[:, :, :, None] * head_scale * carried
    )
    normed = combined * lax.rsqrt(jnp.mean(combined * combined, axis=-1, keepdims=True) + 1e-06)
    attn_rows = jnp.transpose(normed.astype(jnp.bfloat16), (0, 2, 1, 3)).reshape(
        drives_here * tokens_here, heads_here * head_dim
    )
    attn_full = lax.all_gather(attn_rows, "head", axis=1, tiled=True)
    layer_out = jnp.dot(attn_full, out_full, preferred_element_type=jnp.float32).astype(
        jnp.bfloat16
    )
    layer_out = layer_out.reshape(drives_here, rows_here, columns, out_full.shape[1])
    cot_rows = cotangent.reshape(drives_here * tokens_here, cotangent.shape[3])
    factor = float(lax.axis_size("dp") * lax.axis_size("seq") * drives_here * tokens_here) ** (-0.5)
    my_rows = lax.psum_scatter(
        lax.dot_general(
            attn_full, cot_rows, (((0,), (0,)), ((), ())), preferred_element_type=jnp.float32
        )
        * factor,
        "seq",
        scatter_dimension=0,
        tiled=True,
    )
    weight_grad = lax.psum(my_rows, "dp")
    return (layer_out, weight_grad)


def solution(mesh):
    in_specs = (
        P(("groups", "dp"), None, "seq", "head"),
        P(("groups", "dp"), None, "seq", "head"),
        P(("groups", "dp"), None),
        P("seq", None, "head"),
        P("seq", "head"),
        P(("groups", "dp"), "seq", None, "head"),
    )
    out_specs = (P(("groups", "dp"), "seq", None, "head"), P(("groups", "seq"), "head"))
    return jax.shard_map(local, mesh=mesh, in_specs=in_specs, out_specs=out_specs, check_vma=False)
```

profile of v0, /device:TPU:0, one launch (start us, length us, event | category | flops | bytes accessed | tf_op | source)
XLA Modules:
  0.0 310.2 jit_solution(2354458996665151048)
XLA Ops:
  8.0 56.2 %all_to_all.27 = bf16[1,8,128,512]{3,2,0,1:T(8,128)(2,1)S(1)} all-to-all(bf16[1,8,128,512]{3,2,0,1:T(8,128)(2,1)} %bitcast.208), channel_id=1, replica_groups=mesh['groups'=2,'seq'=4,'dp'=2,'head'=2] {'seq'}, dimensions={1} | all-to-all | bytes 2097152 | tf_op jit(solution)/shard_map/all_to_all | solution.py:78
  65.2 5.1 %all-to-all-start = ((bf16[1,8,128,4]{2,3,0,1:T(4,128)(2,1)}), bf16[1,8,128,4]{2,3,0,1:T(4,128)(2,1)S(1)}, u32[]{:S(2)}, u32[]{:S(2)}) async-start(bf16[1,8,128,4]{2,3,0,1:T(4,128)(2,1)} %bitcast.1), calls=%async_computation | async-start | bytes 16384 | tf_op jit(solution)/shard_map/all_to_all | solution.py:79
  74.6 1.4 all-to-all-done
  78.1 13.0 %all-gather.5.cloned.1.call-done = bf16[1024,3,512]{2,0,1:T(8,128)(2,1)} async-done(((bf16[256,3,512]{2,0,1:T(8,128)(2,1)}), bf16[1024,3,512]{2,0,1:T(8,128)(2,1)}) %all-gather.5.cloned.1.call-update) | async-done | bytes 3145744 | tf_op jit(solution)/shard_map/all_gather | solution.py:83
  91.1 4.7 %copy.65 = bf16[1024,3,512]{0,2,1:T(8,128)(2,1)} copy(bf16[1024,3,512]{2,0,1:T(8,128)(2,1)} %all-gather.5.cloned.1.call-done) | data formatting | bytes 6291456 | tf_op jit(solution)/shard_map/all_gather | solution.py:83
  95.8 7.3 %all-gather.7.cloned.1.call-done = bf16[1,2,512,1024]{3,2,1,0:T(8,128)(2,1)} async-done(((bf16[1,2,512,512]{3,2,1,0:T(8,128)(2,1)}), bf16[1,2,512,1024]{3,2,1,0:T(8,128)(2,1)}) %all-gather.7.cloned.1.call-update) | async-done | bytes 2097168 | tf_op jit(solution)/shard_map/all_gather | solution.py:81
  103.1 6.1 %convert_bitcast_fusion = bf16[3,1,4,2,512,128]{4,5,3,2,0,1:T(8,128)(2,1)S(1)} fusion(bf16[1024,3,4,128,1]{0,3,4,2,1:T(8,128)(2,1)} %bitcast.204, bf16[1,2,512,1024]{3,2,1,0:T(8,128)(2,1)} %all-gather.7.cloned.1.call-done), kind=kOutput, calls=%fused_computation.48 | convolution fusion | flops 3222798336 | bytes 8388608 | tf_op jit(solution)/shard_map/bsaf,fchd->cbhsad/dot_general | solution.py:92
  109.2 2.2 fusion.41
  111.4 29.2 %while.24 = (s32[]{:T(128)}, f32[1,4,128,128]{3,2,1,0:T(8,128)S(1)}, f32[2,1,4,512,128]{4,3,2,1,0:T(8,128)}, f32[2,1,4,512]{3,2,1,0:T(4,128)S(1)}, s32[2,1,512]{...) while((s32[]{:T(128)}, ...), condition=%wide.region_6.7_spmd.clone, body=%wide.region_3.6_spmd.clone.sunk | while | flops 1015816256 | bytes 14092170 | solution.py:60
  114.6 3.5 %fusion.69 = f32[4,512,128]{2,1,0:T(8,128)S(1)} fusion(f32[4,512]{1,0:T(4,128)S(1)} %get-tuple-element.263, pred[512,512]{1,0:T(8,128)(4,1)S(1)} %fusion.68, bf16[2,1,4,512,128]{3,4,0,2,1:T(8,128)(2,1)} %get-tuple-element.299, s32[]{:T(128)} %get-tuple-element.279, bf16[2,1,4,512,128]{3,4,0,2,1:T(8,128)(2,1)} %get-tuple-element.298, ...), kind=kOutput, calls=%fused_computation.2.clone.1 | convolution fusion | flops 543162368 | bytes 2901504 | tf_op jit(solution)/shard_map/vmap()/while/body/eval_jaxpr/hts,hsd->htd/dot_general | solution.py:24
  118.1 2.8 fusion.70
  129.2 3.5 %fusion.69 = f32[4,512,128]{2,1,0:T(8,128)S(1)} fusion(f32[4,512]{1,0:T(4,128)S(1)} %get-tuple-element.263, pred[512,512]{1,0:T(8,128)(4,1)S(1)} %fusion.68, bf16[2,1,4,512,128]{3,4,0,2,1:T(8,128)(2,1)} %get-tuple-element.299, s32[]{:T(128)} %get-tuple-element.279, bf16[2,1,4,512,128]{3,4,0,2,1:T(8,128)(2,1)} %get-tuple-element.298, ...), kind=kOutput, calls=%fused_computation.2.clone.1 | convolution fusion | flops 543162368 | bytes 2901504 | tf_op jit(solution)/shard_map/vmap()/while/body/eval_jaxpr/hts,hsd->htd/dot_general | solution.py:24
  132.7 2.8 fusion.70
  140.5 2.9 copy.72
  143.4 2.9 reshape.615
  146.3 1.6 copy.76
  147.9 28.2 %while.23 = (s32[]{:T(128)}, f32[1,4,128,128]{3,2,1,0:T(8,128)S(1)}, f32[1,4]{1,0:T(1,128)S(1)}, f32[1,4,128,128]{3,2,1,0:T(8,128)S(1)}, s32[]{:T(128)}) while((s32[]{:T(128)}, f32[1,4,128,128]{3,2,1,0:T(8,128)S(1)}, f32[1,4]{1,0:T(1,128)S(1)}, f32[1,4,128,128]{3,2,1,0:T(8,128)S(1)}, s32[]{:T(128)}) %tuple.57), condition=%wide.region_10.11_spmd, body=%wide.region_9.10_spmd.sunk | while | flops 131074 | bytes 1835125 | solution.py:115
  148.0 3.7 %collective-permute-start = (f32[1,4,128,128]{3,2,1,0:T(8,128)S(1)}, f32[1,4,128,128]{3,2,1,0:T(8,128)S(1)}, u32[]{:S(2)}, u32[]{:S(2)}) collective-permute-start(f32[1,4,128,128]{3,2,1,0:T(8,128)S(1)} %multiply_add_fusion.3), channel_id=1, source_target_pairs={{0,4},{4,8},{8,12},{1,5},{5,9},{9,13},{2,6},{6,10},{10,14},{3,7},{... | collective-permute-start | bytes 786440 | tf_op jit(solution)/shard_map/while/body/eval_jaxpr/ppermute | solution.py:11
  151.7 6.0 %collective-permute-done = f32[1,4,128,128]{3,2,1,0:T(8,128)S(1)} collective-permute-done((f32[1,4,128,128]{3,2,1,0:T(8,128)S(1)}, f32[1,4,128,128]{3,2,1,0:T(8,128)S(1)}, u32[]{:S(2)}, u32[]{:S(2)}) %collective-permute-start) | collective-permute-done | bytes 262176 | tf_op jit(solution)/shard_map/while/body/eval_jaxpr/ppermute | solution.py:11
  157.8 4.4 %collective-permute-start = (f32[1,4,128,128]{3,2,1,0:T(8,128)S(1)}, f32[1,4,128,128]{3,2,1,0:T(8,128)S(1)}, u32[]{:S(2)}, u32[]{:S(2)}) collective-permute-start(f32[1,4,128,128]{3,2,1,0:T(8,128)S(1)} %multiply_add_fusion.3), channel_id=1, source_target_pairs={{0,4},{4,8},{8,12},{1,5},{5,9},{9,13},{2,6},{6,10},{10,14},{3,7},{... | collective-permute-start | bytes 786440 | tf_op jit(solution)/shard_map/while/body/eval_jaxpr/ppermute | solution.py:11
  162.2 5.2 %collective-permute-done = f32[1,4,128,128]{3,2,1,0:T(8,128)S(1)} collective-permute-done((f32[1,4,128,128]{3,2,1,0:T(8,128)S(1)}, f32[1,4,128,128]{3,2,1,0:T(8,128)S(1)}, u32[]{:S(2)}, u32[]{:S(2)}) %collective-permute-start) | collective-permute-done | bytes 262176 | tf_op jit(solution)/shard_map/while/body/eval_jaxpr/ppermute | solution.py:11
  167.5 4.4 %collective-permute-start = (f32[1,4,128,128]{3,2,1,0:T(8,128)S(1)}, f32[1,4,128,128]{3,2,1,0:T(8,128)S(1)}, u32[]{:S(2)}, u32[]{:S(2)}) collective-permute-start(f32[1,4,128,128]{3,2,1,0:T(8,128)S(1)} %multiply_add_fusion.3), channel_id=1, source_target_pairs={{0,4},{4,8},{8,12},{1,5},{5,9},{9,13},{2,6},{6,10},{10,14},{3,7},{... | collective-permute-start | bytes 786440 | tf_op jit(solution)/shard_map/while/body/eval_jaxpr/ppermute | solution.py:11
  171.9 4.3 %collective-permute-done = f32[1,4,128,128]{3,2,1,0:T(8,128)S(1)} collective-permute-done((f32[1,4,128,128]{3,2,1,0:T(8,128)S(1)}, f32[1,4,128,128]{3,2,1,0:T(8,128)S(1)}, u32[]{:S(2)}, u32[]{:S(2)}) %collective-permute-start) | collective-permute-done | bytes 262176 | tf_op jit(solution)/shard_map/while/body/eval_jaxpr/ppermute | solution.py:11
  176.2 2.9 multiply_reduce_fusion
  179.1 1.2 multiply_convert_fusion.3
  180.4 12.6 %all-gather.9.cloned.1.call-done = bf16[1024,1024]{0,1:T(8,128)(2,1)} async-done(((bf16[1024,512]{0,1:T(8,128)(2,1)}), bf16[1024,1024]{0,1:T(8,128)(2,1)}) %all-gather.9.cloned.1.call-update) | async-done | bytes 2097168 | tf_op jit(solution)/shard_map/all_gather | solution.py:129
  193.0 4.1 %convolution_multiply_fusion.1 = f32[1024,512]{1,0:T(8,128)} fusion(bf16[1024,1024]{0,1:T(8,128)(2,1)} %all-gather.9.cloned.1.call-done, bf16[1024,512]{1,0:T(8,128)(2,1)S(1)} %bitcast.196), kind=kOutput, calls=%fused_computation.53 | convolution fusion | flops 1074266112 | bytes 5242880 | tf_op jit(solution)/shard_map/dot_general | solution.py:137
  197.8 44.5 %reduce-scatter.2.cloned.1.call-done = f32[256,512]{1,0:T(8,128)} async-done(((f32[1024,512]{1,0:T(8,128)}), f32[256,512]{1,0:T(8,128)}) %reduce-scatter.2.cloned.1.call-update) | async-done | bytes 524304 | tf_op jit(solution)/shard_map/reduce_scatter | solution.py:136
  242.4 28.8 %all-gather.11.cloned.1.call-done = bf16[1024,512]{1,0:T(8,128)(2,1)} async-done(((bf16[256,512]{1,0:T(8,128)(2,1)}), bf16[1024,512]{1,0:T(8,128)(2,1)}) %all-gather.11.cloned.1.call-update) | async-done | bytes 1048592 | tf_op jit(solution)/shard_map/all_gather | solution.py:84
  271.1 3.5 %convolution_convert_fusion = bf16[1024,512]{1,0:T(8,128)(2,1)} fusion(bf16[1024,1024]{0,1:T(8,128)(2,1)S(1)} %copy-done.3, bf16[1024,512]{1,0:T(8,128)(2,1)} %all-gather.11.cloned.1.call-done), kind=kOutput, calls=%fused_computation.54 | convolution fusion | flops 1074266112 | bytes 4194304 | tf_op jit(solution)/shard_map/dot_general | solution.py:130
  274.6 26.9 %all-reduce.2.cloned.1.call-done = f32[256,512]{1,0:T(8,128)} async-done(((f32[256,512]{1,0:T(8,128)}), f32[256,512]{1,0:T(8,128)}) %all-reduce.2.cloned.1.call-update) | async-done | bytes 524304 | tf_op jit(solution)/shard_map/psum | solution.py:145
  301.5 1.9 copy.123
  (101 shorter events, 21.8 us)
Async XLA Ops:
  7.2 185.8 %copy-start = (bf16[1,2,512,512]{3,2,1,0:T(8,128)(2,1)S(1)}, bf16[1,2,512,512]{3,2,1,0:T(8,128)(2,1)}, u32[]{:S(2)}) copy-start(bf16[1,2,512,512]{3,2,1,0:T(8,128)(2,1)} %param.15) | copy-start | bytes 3145732
  7.2 83.9 %all-gather.5.cloned.1.call-start = ((), (), s32[]{:S(2)}) async-start(), calls=%async_computation.3 | async-start | bytes 3932160 | tf_op jit(solution)/shard_map/all_gather | solution.py:83
  7.9 95.2 %all-gather.7.cloned.1.call-start = ((), (), s32[]{:S(2)}) async-start(), calls=%async_computation.4 | async-start | bytes 3145728 | tf_op jit(solution)/shard_map/all_gather | solution.py:81
  64.1 6.2 %copy-start.2 = (s32[1,4]{1,0:T(1,128)S(1)}, s32[1,4]{1,0:T(1,128)}, u32[]{:S(2)}) copy-start(s32[1,4]{1,0:T(1,128)} %param.12) | copy-start | bytes 52
  65.2 10.7 %all-to-all-start = ((bf16[1,8,128,4]{2,3,0,1:T(4,128)(2,1)}), bf16[1,8,128,4]{2,3,0,1:T(4,128)(2,1)S(1)}, u32[]{:S(2)}, u32[]{:S(2)}) async-start(bf16[1,8,128,4]{2,3,0,1:T(4,128)(2,1)} %bitcast.1), calls=%async_computation | async-start | bytes 16384 | tf_op jit(solution)/shard_map/all_to_all | solution.py:79
  70.4 122.6 %all-gather.9.cloned.1.call-start = ((), (), s32[]{:S(2)}) async-start(), calls=%async_computation.5 | async-start | bytes 3145728 | tf_op jit(solution)/shard_map/all_gather | solution.py:129
  120.9 4.1 %copy-start.1 = (bf16[2,1,4,512,128]{3,4,0,2,1:T(8,128)(2,1)S(1)}, bf16[2,1,4,512,128]{3,4,0,2,1:T(8,128)(2,1)}, u32[]{:S(2)}) copy-start(bf16[2,1,4,512,128]{3,4,0,2,1:T(8,128)(2,1)} %get-tuple-element.298) | copy-start | bytes 3145732 | tf_op jit(solution)/shard_map/vmap()/while
  135.5 4.1 %copy-start.1 = (bf16[2,1,4,512,128]{3,4,0,2,1:T(8,128)(2,1)S(1)}, bf16[2,1,4,512,128]{3,4,0,2,1:T(8,128)(2,1)}, u32[]{:S(2)}) copy-start(bf16[2,1,4,512,128]{3,4,0,2,1:T(8,128)(2,1)} %get-tuple-element.298) | copy-start | bytes 3145732 | tf_op jit(solution)/shard_map/vmap()/while
  148.0 9.7 %collective-permute-start = (f32[1,4,128,128]{3,2,1,0:T(8,128)S(1)}, f32[1,4,128,128]{3,2,1,0:T(8,128)S(1)}, u32[]{:S(2)}, u32[]{:S(2)}) collective-permute-start(f32[1,4,128,128]{3,2,1,0:T(8,128)S(1)} %multiply_add_fusion.3), channel_id=1, source_target_pairs={{0,4},{4,8},{8,12},{1,5},{5,9},{9,13},{2,6},{6,10},{10,14},{3,7},{... | collective-permute-start | bytes 786440 | tf_op jit(solution)/shard_map/while/body/eval_jaxpr/ppermute | solution.py:11
  157.8 9.6 %collective-permute-start = (f32[1,4,128,128]{3,2,1,0:T(8,128)S(1)}, f32[1,4,128,128]{3,2,1,0:T(8,128)S(1)}, u32[]{:S(2)}, u32[]{:S(2)}) collective-permute-start(f32[1,4,128,128]{3,2,1,0:T(8,128)S(1)} %multiply_add_fusion.3), channel_id=1, source_target_pairs={{0,4},{4,8},{8,12},{1,5},{5,9},{9,13},{2,6},{6,10},{10,14},{3,7},{... | collective-permute-start | bytes 786440 | tf_op jit(solution)/shard_map/while/body/eval_jaxpr/ppermute | solution.py:11
  167.5 8.7 %collective-permute-start = (f32[1,4,128,128]{3,2,1,0:T(8,128)S(1)}, f32[1,4,128,128]{3,2,1,0:T(8,128)S(1)}, u32[]{:S(2)}, u32[]{:S(2)}) collective-permute-start(f32[1,4,128,128]{3,2,1,0:T(8,128)S(1)} %multiply_add_fusion.3), channel_id=1, source_target_pairs={{0,4},{4,8},{8,12},{1,5},{5,9},{9,13},{2,6},{6,10},{10,14},{3,7},{... | collective-permute-start | bytes 786440 | tf_op jit(solution)/shard_map/while/body/eval_jaxpr/ppermute | solution.py:11
  180.3 62.0 %reduce-scatter.2.cloned.1.call-start = ((), (), s32[]{:S(2)}) async-start(), calls=%async_computation.7 | async-start | bytes 2621440 | tf_op jit(solution)/shard_map/reduce_scatter | solution.py:136
  197.1 74.0 %copy-start.3 = (bf16[1024,1024]{0,1:T(8,128)(2,1)S(1)}, bf16[1024,1024]{0,1:T(8,128)(2,1)}, u32[]{:S(2)}) copy-start(bf16[1024,1024]{0,1:T(8,128)(2,1)} %all-gather.9.cloned.1.call-done) | copy-start | bytes 6291460
  197.1 74.0 %all-gather.11.cloned.1.call-start = ((), (), s32[]{:S(2)}) async-start(), calls=%async_computation.6 | async-start | bytes 1310720 | tf_op jit(solution)/shard_map/all_gather | solution.py:84
  197.7 103.8 %all-reduce.2.cloned.1.call-start = ((), (), s32[]{:S(2)}) async-start(), calls=%async_computation.8 | async-start | bytes 1048576 | tf_op jit(solution)/shard_map/psum | solution.py:145
Sparse Core Ops, SparseCore 0:
  9.6 81.4 all-gather.4
  93.2 9.8 all-gather.6
  180.5 12.4 all-gather.8
  197.3 45.0 reduce-scatter.1
  243.8 27.2 all-gather.10
  273.4 28.0 all-reduce.1
where the time goes:
time: 311 us; the launch traced here: 310 us
  waiting for transfers between devices  151 us (49%)
  blocking collectives  56.2 us (18%)
  matrix products  31.1 us (10%)
  local copies, waits for them, and re-layouts  25.4 us (8%)
  starting transfers between devices  17.8 us (6%)
  between operations  15.5 us (5%)
  other arithmetic  10.4 us (3%)
    all_to_all x1, blocking collectives, local(): lax.all_to_all(latents, 'seq', split_axis=1, concat_axis=2, tiled=True)  56.2 us
    reduce_scatter x1, waiting for transfers between devices, local(): lax.psum_scatter(lax.dot_general(attn_full, cot_rows, (((0,), (0,)), ((),...  44.5 us
    all_gather x1, waiting for transfers between devices, local(): lax.all_gather(out_weight, 'seq', axis=0, tiled=True)  28.8 us
    psum x1, waiting for transfers between devices, local(): weight_grad = lax.psum(my_rows, 'dp')  26.9 us
    ppermute x3, waiting for transfers between devices, shifted(): lax.ppermute(value, axis, [(source, source + steps) for source in range(i...  15.4 us
    all_gather x1, waiting for transfers between devices, local(): lax.all_gather(qkv_weight, 'seq', axis=0, tiled=True)  13 us
    all_gather x1, waiting for transfers between devices, local(): attn_full = lax.all_gather(attn_rows, 'head', axis=1, tiled=True)  12.6 us
    ppermute x3, starting transfers between devices, shifted(): lax.ppermute(value, axis, [(source, source + steps) for source in range(i...  12.5 us
  transfers between devices with their start and end apart: 10, of which 10 were waited for; matrix products, arithmetic and copies ran while one was open for 5% of the time, Pallas kernels for 0%

commit v1 on v0

--- a/solution.py
+++ b/solution.py
@@ -3,6 +3,21 @@
 import jax.numpy as jnp
 from jax import lax
 from jax.sharding import PartitionSpec as P
+
+
+def pack_the_edges(vector, a_name):
+    placed, t1 = (jax.lax.axis_size(a_name), jax.lax.axis_index(a_name))
+    w1 = vector.shape[1] // placed
+    value_now = jnp.roll(vector, -t1 * w1, 1)
+    history = [lax.slice_in_dim(value_now, 0, w1, axis=1)]
+    for b in range(1, placed):
+        item_now = lax.slice_in_dim(value_now, b * w1, (b + 1) * w1, axis=1)
+        history.append(
+            jax.lax.ppermute(
+                item_now, a_name, [(to_i, (to_i + b) % placed) for to_i in range(placed)]
+            )
+        )
+    return jnp.roll(jnp.concatenate(history[::-1], 2), (t1 + 1) * history[0].shape[2], 2)
 
 
 def shifted(value, axis, steps):
@@ -76,7 +91,7 @@
 def local(latents, log_decay, seg_lengths, qkv_weight, out_weight, cotangent):
     strips, rate_strips = (
         lax.all_to_all(latents, "seq", split_axis=1, concat_axis=2, tiled=True),
-        lax.all_to_all(log_decay, "seq", split_axis=1, concat_axis=2, tiled=True),
+        pack_the_edges(log_decay, "seq"),
     )
     features = lax.all_gather(strips, "head", axis=3, tiled=True)
     proj_full, out_full = (

time: 311 us -> 311 us (level)
  blocking collectives: 56.2 us -> 0 us
  waiting for transfers between devices: 151 us -> 201 us
  starting transfers between devices: 17.8 us -> 24 us
    all_to_all x1 -> x0, blocking collectives: 56.2 us -> none  [local(): lax.all_to_all(latents, 'seq', split_axis=1, concat_axis=2, tiled=True)]
    all_to_all x1, waiting for transfers between devices: 1.38 us -> 43.7 us  [local(): lax.all_to_all(latents, 'seq', split_axis=1, concat_axis=2, tiled=True)]
    all_gather x1, waiting for transfers between devices: 13 us -> 20.6 us  [local(): lax.all_gather(qkv_weight, 'seq', axis=0, tiled=True)]
    ppermute x0 -> x3, starting transfers between devices: none -> 5 us  [pack_the_edges(): jax.lax.ppermute(item_now, a_name, [(to_i, (to_i + b) % placed) for to_i...]
  transfers between devices with their start and end apart: 10 -> 13, of which waited for: 10 -> 10; matrix products, arithmetic and copies ran while one was open for 5% -> 5% of each run, Pallas kernels for 0% -> 0%
where the time goes in v1:
time: 311 us; the launch traced here: 310 us
  waiting for transfers between devices  201 us (65%)
  matrix products  31 us (10%)
  local copies, waits for them, and re-layouts  25.3 us (8%)
  starting transfers between devices  24 us (8%)
  between operations  15.5 us (5%)
  other arithmetic  10.3 us (3%)
    reduce_scatter x1, waiting for transfers between devices, local(): lax.psum_scatter(lax.dot_general(attn_full, cot_rows, (((0,), (0,)), ((),...  44.5 us
    all_to_all x1, waiting for transfers between devices, local(): lax.all_to_all(latents, 'seq', split_axis=1, concat_axis=2, tiled=True)  43.7 us
    all_gather x1, waiting for transfers between devices, local(): lax.all_gather(out_weight, 'seq', axis=0, tiled=True)  28.8 us
    psum x1, waiting for transfers between devices, local(): weight_grad = lax.psum(my_rows, 'dp')  26.9 us
    all_gather x1, waiting for transfers between devices, local(): lax.all_gather(qkv_weight, 'seq', axis=0, tiled=True)  20.6 us
    ppermute x3, waiting for transfers between devices, shifted(): lax.ppermute(value, axis, [(source, source + steps) for source in range(i...  15.4 us
    all_gather x1, waiting for transfers between devices, local(): attn_full = lax.all_gather(attn_rows, 'head', axis=1, tiled=True)  12.6 us
    ppermute x3, starting transfers between devices, shifted(): lax.ppermute(value, axis, [(source, source + steps) for source in range(i...  12.5 us
  transfers between devices with their start and end apart: 13, of which 10 were waited for; matrix products, arithmetic and copies ran while one was open for 5% of the time, Pallas kernels for 0%

profile of v1, /device:TPU:0, one launch (start us, length us, event | category | flops | bytes accessed | tf_op | source)
XLA Modules:
  0.0 310.1 jit_solution(9616503013667939298)
XLA Ops:
  7.9 6.3 %all-to-all-start = ((bf16[1,8,128,512]{3,2,0,1:T(8,128)(2,1)}), bf16[1,8,128,512]{3,2,0,1:T(8,128)(2,1)S(1)}, u32[]{:S(2)}, u32[]{:S(2)}) async-start(bf16[1,8,128,512]{3,2,0,1:T(8,128)(2,1)} %bitcast.205), calls=%async_computation | async-start | bytes 2097152 | tf_op jit(solution)/shard_map/all_to_all | solution.py:93
  14.3 3.9 %collective-permute-start.1 = (bf16[1,2,128,4]{2,3,0,1:T(4,128)(2,1)S(1)}, bf16[1,2,128,4]{2,3,0,1:T(4,128)(2,1)S(1)}, u32[]{:S(2)}, u32[]{:S(2)}) collective-permute-start(bf16[1,2,128,4]{2,3,0,1:T(4,128)(2,1)S(1)} %get-tuple-element.179), channel_id=1, source_target_pairs={{0,12},{4,0},{8,4},{12,8},{1,13},{5,1},{9,5},{13,9},{2,14},{6,2},{... | collective-permute-start | bytes 6152 | tf_op jit(solution)/shard_map/ppermute | solution.py:16
  21.5 43.7 %all-to-all-done = bf16[1,8,128,512]{3,2,0,1:T(8,128)(2,1)S(1)} async-done(((bf16[1,8,128,512]{3,2,0,1:T(8,128)(2,1)}), bf16[1,8,128,512]{3,2,0,1:T(8,128)(2,1)S(1)}, u32[]{:S(2)}, u32[]{:S(2)}) %all-to-all-start) | async-done | bytes 1048608 | tf_op jit(solution)/shard_map/all_to_all | solution.py:93
  70.4 20.6 %all-gather.5.cloned.1.call-done = bf16[1024,3,512]{2,0,1:T(8,128)(2,1)} async-done(((bf16[256,3,512]{2,0,1:T(8,128)(2,1)}), bf16[1024,3,512]{2,0,1:T(8,128)(2,1)}) %all-gather.5.cloned.1.call-update) | async-done | bytes 3145744 | tf_op jit(solution)/shard_map/all_gather | solution.py:98
  91.1 4.7 %copy.67 = bf16[1024,3,512]{0,2,1:T(8,128)(2,1)} copy(bf16[1024,3,512]{2,0,1:T(8,128)(2,1)} %all-gather.5.cloned.1.call-done) | data formatting | bytes 6291456 | tf_op jit(solution)/shard_map/all_gather | solution.py:98
  95.8 7.4 %all-gather.7.cloned.1.call-done = bf16[1,2,512,1024]{3,2,1,0:T(8,128)(2,1)} async-done(((bf16[1,2,512,512]{3,2,1,0:T(8,128)(2,1)}), bf16[1,2,512,1024]{3,2,1,0:T(8,128)(2,1)}) %all-gather.7.cloned.1.call-update) | async-done | bytes 2097168 | tf_op jit(solution)/shard_map/all_gather | solution.py:96
  103.2 6.0 %convert_bitcast_fusion = bf16[3,1,4,2,512,128]{4,5,3,2,0,1:T(8,128)(2,1)S(1)} fusion(bf16[1024,3,4,128,1]{0,3,4,2,1:T(8,128)(2,1)} %bitcast.201, bf16[1,2,512,1024]{3,2,1,0:T(8,128)(2,1)} %all-gather.7.cloned.1.call-done), kind=kOutput, calls=%fused_computation.48 | convolution fusion | flops 3222798336 | bytes 8388608 | tf_op jit(solution)/shard_map/bsaf,fchd->cbhsad/dot_general | solution.py:107
  109.2 2.2 fusion.42
  111.4 29.0 %while.24 = (s32[]{:T(128)}, f32[1,4,128,128]{3,2,1,0:T(8,128)S(1)}, f32[2,1,4,512,128]{4,3,2,1,0:T(8,128)}, f32[2,1,4,512]{3,2,1,0:T(4,128)S(1)}, s32[2,1,512]{...) while((s32[]{:T(128)}, ...), condition=%wide.region_6.7_spmd.clone, body=%wide.region_3.6_spmd.clone.sunk | while | flops 1015816256 | bytes 14092170 | solution.py:75
  114.7 3.5 %fusion.71 = f32[4,512,128]{2,1,0:T(8,128)S(1)} fusion(f32[4,512]{1,0:T(4,128)S(1)} %get-tuple-element.268, pred[512,512]{1,0:T(8,128)(4,1)S(1)} %fusion.70, bf16[2,1,4,512,128]{3,4,0,2,1:T(8,128)(2,1)} %get-tuple-element.304, s32[]{:T(128)} %get-tuple-element.284, bf16[2,1,4,512,128]{3,4,0,2,1:T(8,128)(2,1)} %get-tuple-element.303, ...), kind=kOutput, calls=%fused_computation.2.clone.1 | convolution fusion | flops 543162368 | bytes 2901504 | tf_op jit(solution)/shard_map/vmap()/while/body/eval_jaxpr/hts,hsd->htd/dot_general | solution.py:39
  118.3 2.8 fusion.72
  129.3 3.5 %fusion.71 = f32[4,512,128]{2,1,0:T(8,128)S(1)} fusion(f32[4,512]{1,0:T(4,128)S(1)} %get-tuple-element.268, pred[512,512]{1,0:T(8,128)(4,1)S(1)} %fusion.70, bf16[2,1,4,512,128]{3,4,0,2,1:T(8,128)(2,1)} %get-tuple-element.304, s32[]{:T(128)} %get-tuple-element.284, bf16[2,1,4,512,128]{3,4,0,2,1:T(8,128)(2,1)} %get-tuple-element.303, ...), kind=kOutput, calls=%fused_computation.2.clone.1 | convolution fusion | flops 543162368 | bytes 2901504 | tf_op jit(solution)/shard_map/vmap()/while/body/eval_jaxpr/hts,hsd->htd/dot_general | solution.py:39
  132.8 2.8 fusion.72
  140.5 2.9 copy.74
  143.3 2.9 reshape.599
  146.2 1.6 copy.78
  147.8 28.2 %while.23 = (s32[]{:T(128)}, f32[1,4,128,128]{3,2,1,0:T(8,128)S(1)}, f32[1,4]{1,0:T(1,128)S(1)}, f32[1,4,128,128]{3,2,1,0:T(8,128)S(1)}, s32[]{:T(128)}) while((s32[]{:T(128)}, f32[1,4,128,128]{3,2,1,0:T(8,128)S(1)}, f32[1,4]{1,0:T(1,128)S(1)}, f32[1,4,128,128]{3,2,1,0:T(8,128)S(1)}, s32[]{:T(128)}) %tuple.60), condition=%wide.region_10.11_spmd, body=%wide.region_9.10_spmd.sunk | while | flops 131074 | bytes 1835125 | solution.py:130
  148.0 3.7 %collective-permute-start = (f32[1,4,128,128]{3,2,1,0:T(8,128)S(1)}, f32[1,4,128,128]{3,2,1,0:T(8,128)S(1)}, u32[]{:S(2)}, u32[]{:S(2)}) collective-permute-start(f32[1,4,128,128]{3,2,1,0:T(8,128)S(1)} %multiply_add_fusion.3), channel_id=1, source_target_pairs={{0,4},{4,8},{8,12},{1,5},{5,9},{9,13},{2,6},{6,10},{10,14},{3,7},{... | collective-permute-start | bytes 786440 | tf_op jit(solution)/shard_map/while/body/eval_jaxpr/ppermute | solution.py:26
  151.6 6.0 %collective-permute-done = f32[1,4,128,128]{3,2,1,0:T(8,128)S(1)} collective-permute-done((f32[1,4,128,128]{3,2,1,0:T(8,128)S(1)}, f32[1,4,128,128]{3,2,1,0:T(8,128)S(1)}, u32[]{:S(2)}, u32[]{:S(2)}) %collective-permute-start) | collective-permute-done | bytes 262176 | tf_op jit(solution)/shard_map/while/body/eval_jaxpr/ppermute | solution.py:26
  157.7 4.4 %collective-permute-start = (f32[1,4,128,128]{3,2,1,0:T(8,128)S(1)}, f32[1,4,128,128]{3,2,1,0:T(8,128)S(1)}, u32[]{:S(2)}, u32[]{:S(2)}) collective-permute-start(f32[1,4,128,128]{3,2,1,0:T(8,128)S(1)} %multiply_add_fusion.3), channel_id=1, source_target_pairs={{0,4},{4,8},{8,12},{1,5},{5,9},{9,13},{2,6},{6,10},{10,14},{3,7},{... | collective-permute-start | bytes 786440 | tf_op jit(solution)/shard_map/while/body/eval_jaxpr/ppermute | solution.py:26
  162.1 5.2 %collective-permute-done = f32[1,4,128,128]{3,2,1,0:T(8,128)S(1)} collective-permute-done((f32[1,4,128,128]{3,2,1,0:T(8,128)S(1)}, f32[1,4,128,128]{3,2,1,0:T(8,128)S(1)}, u32[]{:S(2)}, u32[]{:S(2)}) %collective-permute-start) | collective-permute-done | bytes 262176 | tf_op jit(solution)/shard_map/while/body/eval_jaxpr/ppermute | solution.py:26
  167.4 4.4 %collective-permute-start = (f32[1,4,128,128]{3,2,1,0:T(8,128)S(1)}, f32[1,4,128,128]{3,2,1,0:T(8,128)S(1)}, u32[]{:S(2)}, u32[]{:S(2)}) collective-permute-start(f32[1,4,128,128]{3,2,1,0:T(8,128)S(1)} %multiply_add_fusion.3), channel_id=1, source_target_pairs={{0,4},{4,8},{8,12},{1,5},{5,9},{9,13},{2,6},{6,10},{10,14},{3,7},{... | collective-permute-start | bytes 786440 | tf_op jit(solution)/shard_map/while/body/eval_jaxpr/ppermute | solution.py:26
  171.8 4.3 %collective-permute-done = f32[1,4,128,128]{3,2,1,0:T(8,128)S(1)} collective-permute-done((f32[1,4,128,128]{3,2,1,0:T(8,128)S(1)}, f32[1,4,128,128]{3,2,1,0:T(8,128)S(1)}, u32[]{:S(2)}, u32[]{:S(2)}) %collective-permute-start) | collective-permute-done | bytes 262176 | tf_op jit(solution)/shard_map/while/body/eval_jaxpr/ppermute | solution.py:26
  176.1 2.9 multiply_reduce_fusion
  179.0 1.2 multiply_convert_fusion.3
  180.3 12.6 %all-gather.9.cloned.1.call-done = bf16[1024,1024]{0,1:T(8,128)(2,1)} async-done(((bf16[1024,512]{0,1:T(8,128)(2,1)}), bf16[1024,1024]{0,1:T(8,128)(2,1)}) %all-gather.9.cloned.1.call-update) | async-done | bytes 2097168 | tf_op jit(solution)/shard_map/all_gather | solution.py:144
  192.9 4.1 %convolution_multiply_fusion.1 = f32[1024,512]{1,0:T(8,128)} fusion(bf16[1024,1024]{0,1:T(8,128)(2,1)} %all-gather.9.cloned.1.call-done, bf16[1024,512]{1,0:T(8,128)(2,1)S(1)} %bitcast.193), kind=kOutput, calls=%fused_computation.53 | convolution fusion | flops 1074266112 | bytes 5242880 | tf_op jit(solution)/shard_map/dot_general | solution.py:152
  197.7 44.5 %reduce-scatter.2.cloned.1.call-done = f32[256,512]{1,0:T(8,128)} async-done(((f32[1024,512]{1,0:T(8,128)}), f32[256,512]{1,0:T(8,128)}) %reduce-scatter.2.cloned.1.call-update) | async-done | bytes 524304 | tf_op jit(solution)/shard_map/reduce_scatter | solution.py:151
  242.3 28.8 %all-gather.11.cloned.1.call-done = bf16[1024,512]{1,0:T(8,128)(2,1)} async-done(((bf16[256,512]{1,0:T(8,128)(2,1)}), bf16[1024,512]{1,0:T(8,128)(2,1)}) %all-gather.11.cloned.1.call-update) | async-done | bytes 1048592 | tf_op jit(solution)/shard_map/all_gather | solution.py:99
  271.0 3.5 %convolution_convert_fusion = bf16[1024,512]{1,0:T(8,128)(2,1)} fusion(bf16[1024,1024]{0,1:T(8,128)(2,1)S(1)} %copy-done.4, bf16[1024,512]{1,0:T(8,128)(2,1)} %all-gather.11.cloned.1.call-done), kind=kOutput, calls=%fused_computation.54 | convolution fusion | flops 1074266112 | bytes 4194304 | tf_op jit(solution)/shard_map/dot_general | solution.py:145
  274.5 26.9 %all-reduce.2.cloned.1.call-done = f32[256,512]{1,0:T(8,128)} async-done(((f32[256,512]{1,0:T(8,128)}), f32[256,512]{1,0:T(8,128)}) %all-reduce.2.cloned.1.call-update) | async-done | bytes 524304 | tf_op jit(solution)/shard_map/psum | solution.py:160
  301.4 1.9 copy.132
  (116 shorter events, 22.7 us)
Async XLA Ops:
  7.2 185.7 %copy-start = (bf16[1,2,512,512]{3,2,1,0:T(8,128)(2,1)S(1)}, bf16[1,2,512,512]{3,2,1,0:T(8,128)(2,1)}, u32[]{:S(2)}) copy-start(bf16[1,2,512,512]{3,2,1,0:T(8,128)(2,1)} %param.15) | copy-start | bytes 3145732
  7.2 7.1 %copy-start.2 = (bf16[1,8,128,4]{2,3,1,0:T(4,128)(2,1)S(1)}, bf16[1,8,128,4]{2,3,1,0:T(4,128)(2,1)}, u32[]{:S(2)}) copy-start(bf16[1,8,128,4]{2,3,1,0:T(4,128)(2,1)} %param.11) | copy-start | bytes 24580
  7.2 12.2 %copy-start.3 = (s32[1,4]{1,0:T(1,128)S(1)}, s32[1,4]{1,0:T(1,128)}, u32[]{:S(2)}) copy-start(s32[1,4]{1,0:T(1,128)} %param.12) | copy-start | bytes 52
  7.2 83.9 %all-gather.5.cloned.1.call-start = ((), (), s32[]{:S(2)}) async-start(), calls=%async_computation.2 | async-start | bytes 3932160 | tf_op jit(solution)/shard_map/all_gather | solution.py:98
  7.9 57.3 %all-to-all-start = ((bf16[1,8,128,512]{3,2,0,1:T(8,128)(2,1)}), bf16[1,8,128,512]{3,2,0,1:T(8,128)(2,1)S(1)}, u32[]{:S(2)}, u32[]{:S(2)}) async-start(bf16[1,8,128,512]{3,2,0,1:T(8,128)(2,1)} %bitcast.205), calls=%async_computation | async-start | bytes 2097152 | tf_op jit(solution)/shard_map/all_to_all | solution.py:93
  14.3 88.9 %all-gather.7.cloned.1.call-start = ((), (), s32[]{:S(2)}) async-start(), calls=%async_computation.3 | async-start | bytes 3145728 | tf_op jit(solution)/shard_map/all_gather | solution.py:96
  14.3 53.8 %collective-permute-start.1 = (bf16[1,2,128,4]{2,3,0,1:T(4,128)(2,1)S(1)}, bf16[1,2,128,4]{2,3,0,1:T(4,128)(2,1)S(1)}, u32[]{:S(2)}, u32[]{:S(2)}) collective-permute-start(bf16[1,2,128,4]{2,3,0,1:T(4,128)(2,1)S(1)} %get-tuple-element.179), channel_id=1, source_target_pairs={{0,12},{4,0},{8,4},{12,8},{1,13},{5,1},{9,5},{13,9},{2,14},{6,2},{... | collective-permute-start | bytes 6152 | tf_op jit(solution)/shard_map/ppermute | solution.py:16
  18.2 49.9 %collective-permute-start.2 = (bf16[1,2,128,4]{2,3,0,1:T(4,128)(2,1)S(1)}, bf16[1,2,128,4]{2,3,0,1:T(4,128)(2,1)S(1)}, u32[]{:S(2)}, u32[]{:S(2)}) collective-permute-start(bf16[1,2,128,4]{2,3,0,1:T(4,128)(2,1)S(1)} %get-tuple-element.178), channel_id=1, source_target_pairs={{0,8},{4,12},{8,0},{12,4},{1,9},{5,13},{9,1},{13,5},{2,10},{6,14},... | collective-permute-start | bytes 6152 | tf_op jit(solution)/shard_map/ppermute | solution.py:16
  18.2 50.0 %collective-permute-start.3 = (bf16[1,2,128,4]{2,3,0,1:T(4,128)(2,1)S(1)}, bf16[1,2,128,4]{2,3,0,1:T(4,128)(2,1)S(1)}, u32[]{:S(2)}, u32[]{:S(2)}) collective-permute-start(bf16[1,2,128,4]{2,3,0,1:T(4,128)(2,1)S(1)} %get-tuple-element.177), channel_id=1, source_target_pairs={{0,4},{4,8},{8,12},{12,0},{1,5},{5,9},{9,13},{13,1},{2,6},{6,10},{... | collective-permute-start | bytes 6152 | tf_op jit(solution)/shard_map/ppermute | solution.py:16
  66.3 126.6 %all-gather.9.cloned.1.call-start = ((), (), s32[]{:S(2)}) async-start(), calls=%async_computation.4 | async-start | bytes 3145728 | tf_op jit(solution)/shard_map/all_gather | solution.py:144
  121.1 3.9 %copy-start.1 = (bf16[2,1,4,512,128]{3,4,0,2,1:T(8,128)(2,1)S(1)}, bf16[2,1,4,512,128]{3,4,0,2,1:T(8,128)(2,1)}, u32[]{:S(2)}) copy-start(bf16[2,1,4,512,128]{3,4,0,2,1:T(8,128)(2,1)} %get-tuple-element.303) | copy-start | bytes 3145732 | tf_op jit(solution)/shard_map/vmap()/while
  135.6 3.9 %copy-start.1 = (bf16[2,1,4,512,128]{3,4,0,2,1:T(8,128)(2,1)S(1)}, bf16[2,1,4,512,128]{3,4,0,2,1:T(8,128)(2,1)}, u32[]{:S(2)}) copy-start(bf16[2,1,4,512,128]{3,4,0,2,1:T(8,128)(2,1)} %get-tuple-element.303) | copy-start | bytes 3145732 | tf_op jit(solution)/shard_map/vmap()/while
  148.0 9.7 %collective-permute-start = (f32[1,4,128,128]{3,2,1,0:T(8,128)S(1)}, f32[1,4,128,128]{3,2,1,0:T(8,128)S(1)}, u32[]{:S(2)}, u32[]{:S(2)}) collective-permute-start(f32[1,4,128,128]{3,2,1,0:T(8,128)S(1)} %multiply_add_fusion.3), channel_id=1, source_target_pairs={{0,4},{4,8},{8,12},{1,5},{5,9},{9,13},{2,6},{6,10},{10,14},{3,7},{... | collective-permute-start | bytes 786440 | tf_op jit(solution)/shard_map/while/body/eval_jaxpr/ppermute | solution.py:26
  157.7 9.6 %collective-permute-start = (f32[1,4,128,128]{3,2,1,0:T(8,128)S(1)}, f32[1,4,128,128]{3,2,1,0:T(8,128)S(1)}, u32[]{:S(2)}, u32[]{:S(2)}) collective-permute-start(f32[1,4,128,128]{3,2,1,0:T(8,128)S(1)} %multiply_add_fusion.3), channel_id=1, source_target_pairs={{0,4},{4,8},{8,12},{1,5},{5,9},{9,13},{2,6},{6,10},{10,14},{3,7},{... | collective-permute-start | bytes 786440 | tf_op jit(solution)/shard_map/while/body/eval_jaxpr/ppermute | solution.py:26
  167.4 8.7 %collective-permute-start = (f32[1,4,128,128]{3,2,1,0:T(8,128)S(1)}, f32[1,4,128,128]{3,2,1,0:T(8,128)S(1)}, u32[]{:S(2)}, u32[]{:S(2)}) collective-permute-start(f32[1,4,128,128]{3,2,1,0:T(8,128)S(1)} %multiply_add_fusion.3), channel_id=1, source_target_pairs={{0,4},{4,8},{8,12},{1,5},{5,9},{9,13},{2,6},{6,10},{10,14},{3,7},{... | collective-permute-start | bytes 786440 | tf_op jit(solution)/shard_map/while/body/eval_jaxpr/ppermute | solution.py:26
  180.2 62.0 %reduce-scatter.2.cloned.1.call-start = ((), (), s32[]{:S(2)}) async-start(), calls=%async_computation.6 | async-start | bytes 2621440 | tf_op jit(solution)/shard_map/reduce_scatter | solution.py:151
  197.0 74.0 %copy-start.4 = (bf16[1024,1024]{0,1:T(8,128)(2,1)S(1)}, bf16[1024,1024]{0,1:T(8,128)(2,1)}, u32[]{:S(2)}) copy-start(bf16[1024,1024]{0,1:T(8,128)(2,1)} %all-gather.9.cloned.1.call-done) | copy-start | bytes 6291460
  197.1 74.0 %all-gather.11.cloned.1.call-start = ((), (), s32[]{:S(2)}) async-start(), calls=%async_computation.5 | async-start | bytes 1310720 | tf_op jit(solution)/shard_map/all_gather | solution.py:99
  197.7 103.8 %all-reduce.2.cloned.1.call-start = ((), (), s32[]{:S(2)}) async-start(), calls=%async_computation.7 | async-start | bytes 1048576 | tf_op jit(solution)/shard_map/psum | solution.py:160
Sparse Core Ops, SparseCore 0:
  9.6 81.4 all-gather.4
  93.2 9.9 all-gather.6
  180.4 12.4 all-gather.8
  197.2 45.0 reduce-scatter.1
  243.7 27.2 all-gather.10
  273.3 28.0 all-reduce.1
